TPU v7x, 32 devices: a whole 2x2x4 slice. The times are simulated.
32 devices in a mesh: freq: 2 (over y), cell: 4 (over z), sub: 4 (over x, core).
Axes of the slice: x: 2, y: 2, z: 4, core: 2. Of those that a mesh axis runs over, the one named last changes fastest.
Arguments:
- direction: float32 [4, 240, 2048], P('freq', 'sub', 'cell'), parts along dimension 0, may hold values from -6 to 6
- neighbours: int32 [12, 2048], P(None, 'cell'), may hold values from 0 to 2047, as said below
- spacing: float32 [12, 2048], P(None, 'cell'), may hold values from 1 to 3
- scatterer: int32 [2048, 1], P('cell'), may hold values from 0 to 15; in each aligned block of 512 rows (0 to 511, 512 to 1023, ...) at most 128 rows name the same one
- box_index: int32 [2048], P('cell'), may hold values from 0 to 63, as said below
- translation: float32 [16, 240, 480], P(None, 'sub', 'freq'), parts along dimension 2, may hold values from -0.046875 to 0.046875
- response: float32 [16, 240, 480], P('cell', 'sub', 'freq'), parts along dimension 2, may hold values from -0.375 to 0.375
- coarse_map: float32 [240, 480], P('sub', 'freq'), parts along dimension 1, may hold values from -0.015625 to 0.015625
Outputs:
- product: float32 [4, 240, 2048], P('freq', 'sub', 'cell'), parts along dimension 0
There are 2 independent parts, one for each index of `freq`. A program takes and returns all parts, laid end to end along the dimension named above; an argument that names none is the same for every part. Nothing has to cross between parts.
Inputs may be any that keep to these rules, and one draw needn't show every extreme that they name: neighbours[n, i] differs from i by 1 to 128; neighbours[0, i] differs from i by exactly 128. `box_index`: non-decreasing; the j-th block of 512 meta-atoms holds exactly the boxes j * 16 to (j + 1) * 16 - 1, each with one meta-atom or more. `scatterer`: among the meta-atoms of one index of cell no type occurs more than 128 times.
All inputs are finite; a program needn't handle non-finite values.
Results may differ from a plain program's by a relative error of at most 0.000052.
Values sent between devices are 32-bit elements; how exact they have to be, the bound alone decides.
A program may use at most 64 MiB of HBM per device.

v0:
```python
import jax
import jax.numpy as jnp
from jax import lax
from jax.sharding import PartitionSpec as P

NB = 12
QTERMS = 16
BOX_DEV = 16
WIN = 128


def with_halo(x, sides, width):
    for axis, dim in sides:
        size, length = (lax.axis_size(axis), x.shape[dim])
        up = [(i, (i + 1) % size) for i in range(size - 1)]
        down = [(j, i) for i, j in up]
        last = lax.slice_in_dim(x, length - width, length, axis=dim)
        first = lax.slice_in_dim(x, 0, width, axis=dim)
        before = lax.ppermute(last, axis, up)
        after = lax.ppermute(first, axis, down)
        x = jnp.concatenate([before, x, after], axis=dim)
    return x


def coupling(distance):
    orders = jnp.arange(QTERMS).astype(jnp.float32)
    return jnp.cos(0.9 * orders[None, :, None] * distance[:, None, :]) / distance[:, None, :]


def finish(pieces, response):
    highest = lax.Precision.HIGHEST
    total = jnp.einsum("trc,xtmkc->xtmkr", response, pieces, precision=highest)
    return lax.all_to_all(total, "cell", split_axis=0, concat_axis=0, tiled=True)


def on_device(
    direction, neighbours, spacing, scatterer, box_index, translation, response, coarse_map
):
    highest = lax.Precision.HIGHEST
    nrhs_count, rows_own, atom_count = direction.shape
    full_rows = translation.shape[2]
    term_count = translation.shape[0]
    cell_count = lax.axis_size("cell")
    cell_id = lax.axis_index("cell")
    gathered = lax.all_gather(direction, "sub", axis=1, tiled=True)
    weights = coupling(spacing)
    local_index = neighbours - (cell_id * atom_count - WIN)
    rows_first = jnp.transpose(gathered, (2, 0, 1))
    extended = with_halo(rows_first, (("cell", 0),), WIN)

    def add_pair(step, total):
        picked = jnp.take(extended, local_index[step], axis=0)
        return total + weights[step][:, :, None, None] * picked[None]

    mixed = lax.fori_loop(
        0, NB, add_pair, jnp.zeros((term_count, atom_count, nrhs_count, full_rows), jnp.float32)
    )
    near = jnp.einsum("qrc,qakc->kra", translation, mixed, precision=highest)
    first_box = cell_id * BOX_DEV
    membership = (
        box_index[None, :] - first_box == jnp.arange(BOX_DEV, dtype=jnp.int32)[:, None]
    ).astype(jnp.float32)
    box_sums = jnp.einsum("kra,da->krd", direction, membership, precision=highest)
    all_sums = lax.all_gather(box_sums, "cell", axis=2, tiled=True)
    every_box = jnp.arange(BOX_DEV * cell_count, dtype=jnp.int32)
    own_boxes = first_box + jnp.arange(BOX_DEV, dtype=jnp.int32)
    offsets = (every_box[:, None] - own_boxes[None, :]).astype(jnp.float32)
    kernel = jnp.where(
        offsets == 0.0,
        jnp.float32(0.0),
        jnp.cos(1.3 * offsets) / jnp.sqrt(jnp.maximum(jnp.abs(offsets), 1.0)),
    )
    local = jnp.einsum("krb,bd->krd", all_sums, kernel, precision=highest)
    local_full = lax.all_gather(local, "sub", axis=1, tiled=True)
    far_box = jnp.einsum("rc,kcd->krd", coarse_map, local_full, precision=highest)
    far = jnp.einsum("krd,da->kra", far_box, membership, precision=highest)
    incident = near + far
    type_count = response.shape[0]
    most = atom_count // 32 * max(1, 32 // cell_count)
    slots = type_count * most
    kinds = scatterer[:, 0]
    owner = kinds // type_count
    local_kind = kinds % type_count
    atom_ids = jnp.arange(atom_count, dtype=jnp.int32)
    earlier = (kinds[:, None] == kinds[None, :]) & (atom_ids[:, None] > atom_ids[None, :])
    position = jnp.sum(earlier.astype(jnp.int32), axis=1)
    target = owner * slots + local_kind * most + position
    field_full = lax.all_gather(incident, "sub", axis=1, tiled=True)
    field_rows = jnp.transpose(field_full, (2, 0, 1))
    placed = (
        jnp.zeros((cell_count * slots, nrhs_count, full_rows), jnp.float32)
        .at[target]
        .set(field_rows)
    )
    outgoing = placed.reshape(cell_count, type_count, most, nrhs_count, full_rows)
    returned = finish(
        lax.all_to_all(outgoing, "cell", split_axis=0, concat_axis=0, tiled=True), response
    )
    flat_return = returned.reshape(cell_count * slots, nrhs_count, rows_own)
    scattered_rows = jnp.take(flat_return, target, axis=0)
    scattered = jnp.transpose(scattered_rows, (1, 2, 0))
    return direction - scattered


def solution(mesh):
    in_specs = (
        P("freq", "sub", "cell"),
        P(None, "cell"),
        P(None, "cell"),
        P("cell", None),
        P("cell"),
        P(None, "sub", "freq"),
        P("cell", "sub", "freq"),
        P("sub", "freq"),
    )
    out_specs = P("freq", "sub", "cell")
    return jax.shard_map(
        on_device, mesh=mesh, in_specs=in_specs, out_specs=out_specs, check_vma=False
    )
```

profile of v0, /device:TPU:0, one launch (start us, length us, event | category | flops | bytes accessed | tf_op | source)
XLA Modules:
  0.0 495.5 jit_solution(50812902480453405)
XLA Ops:
  0.0 11.4 %all_gather.12 = f32[2,240,512]{2,0,1:T(2,128)S(1)} all-gather(f32[2,60,512]{2,0,1:T(2,128)} %param.10), channel_id=1, replica_groups=mesh['freq'=2,'cell'=4,'sub'=4] {'sub'}, dimensions={1}, use_global_device_ids=true | all-gather | bytes 1228800 | tf_op jit(solution)/shard_map/all_gather | solution.py:45
  11.6 3.5 collective-permute-start
  18.4 15.9 %all_gather.13 = f32[2,60,64]{1,0,2:T(2,128)S(1)} all-gather(f32[2,60,16]{1,0,2:T(2,128)S(1)} %copy.66), channel_id=1, replica_groups=mesh['freq'=2,'cell'=4,'sub'=4] {'cell'}, dimensions={2}, use_global_device_ids=true | all-gather | bytes 38400 | tf_op jit(solution)/shard_map/all_gather | solution.py:64
  34.6 5.7 %all_gather.14 = f32[2,240,16]{2,0,1:T(2,128)S(1)} all-gather(f32[2,60,16]{2,0,1:T(2,128)S(1)} %copy.68), channel_id=1, replica_groups=mesh['freq'=2,'cell'=4,'sub'=4] {'sub'}, dimensions={1}, use_global_device_ids=true | all-gather | bytes 38400 | tf_op jit(solution)/shard_map/all_gather | solution.py:74
  44.2 2.9 cosine_divide_fusion
  47.7 2.9 copy.62
  50.7 225.0 %while.14 = (s32[]{:T(128)}, f32[16,512,2,240]{3,2,1,0:T(2,128)}, f32[12,16,512]{2,1,0:T(8,128)}, s32[12,512]{1,0:T(8,128)S(1)}, f32[768,2,240]{2,1,0:T(2,128)}, /*index=5*/s32[]{:T(128)}, s32[]{:T(128)}) while((s32[]{:T(128)}, f32[16,512,2,240]{3,2,1,0:T(2,128)}, f32[12,16,512]{2,1,0:T(8,128)}, s32[12,512]{1,0:T(8,128)S(1)}, ...), condition=%wide.region_2.3_spmd.clone, body=%wide.region_1.0_spmd.clone.sunk | while | flops 12047875 | bytes 36488284 | solution.py:55
  50.7 3.5 gather_fusion
  54.2 1.8 broadcast_select_fusion.2
  56.8 11.8 %select_add_fusion.2 = f32[16,512,2,240]{3,2,1,0:T(2,128)} fusion(f32[16,512,2,240]{3,2,1,0:T(2,128)} %get-tuple-element.192, pred[]{:T(512)S(6)} %compare.10, f32[512,2,240]{2,1,0:T(2,128)S(1)} %broadcast_select_fusion.2, f32[16,512]{1,0:T(8,128)S(1)} %dynamic-slice_bitcast_fusion.2), kind=kLoop, calls=%fused_computation.3.clone.1 | loop fusion | flops 11796480 | bytes 32473088 | tf_op jit(solution)/shard_map/while/body/eval_jaxpr/add | solution.py:53
  68.6 3.4 gather_fusion
  72.0 1.8 broadcast_select_fusion.2
  74.5 12.8 %select_add_fusion.2 = f32[16,512,2,240]{3,2,1,0:T(2,128)} fusion(f32[16,512,2,240]{3,2,1,0:T(2,128)} %get-tuple-element.192, pred[]{:T(512)S(6)} %compare.10, f32[512,2,240]{2,1,0:T(2,128)S(1)} %broadcast_select_fusion.2, f32[16,512]{1,0:T(8,128)S(1)} %dynamic-slice_bitcast_fusion.2), kind=kLoop, calls=%fused_computation.3.clone.1 | loop fusion | flops 11796480 | bytes 32473088 | tf_op jit(solution)/shard_map/while/body/eval_jaxpr/add | solution.py:53
  87.4 3.4 gather_fusion
  90.8 1.8 broadcast_select_fusion.2
  93.4 12.8 %select_add_fusion.2 = f32[16,512,2,240]{3,2,1,0:T(2,128)} fusion(f32[16,512,2,240]{3,2,1,0:T(2,128)} %get-tuple-element.192, pred[]{:T(512)S(6)} %compare.10, f32[512,2,240]{2,1,0:T(2,128)S(1)} %broadcast_select_fusion.2, f32[16,512]{1,0:T(8,128)S(1)} %dynamic-slice_bitcast_fusion.2), kind=kLoop, calls=%fused_computation.3.clone.1 | loop fusion | flops 11796480 | bytes 32473088 | tf_op jit(solution)/shard_map/while/body/eval_jaxpr/add | solution.py:53
  106.2 3.4 gather_fusion
  109.7 1.8 broadcast_select_fusion.2
  112.2 12.8 %select_add_fusion.2 = f32[16,512,2,240]{3,2,1,0:T(2,128)} fusion(f32[16,512,2,240]{3,2,1,0:T(2,128)} %get-tuple-element.192, pred[]{:T(512)S(6)} %compare.10, f32[512,2,240]{2,1,0:T(2,128)S(1)} %broadcast_select_fusion.2, f32[16,512]{1,0:T(8,128)S(1)} %dynamic-slice_bitcast_fusion.2), kind=kLoop, calls=%fused_computation.3.clone.1 | loop fusion | flops 11796480 | bytes 32473088 | tf_op jit(solution)/shard_map/while/body/eval_jaxpr/add | solution.py:53
  125.1 3.4 gather_fusion
  131.0 12.8 %select_add_fusion.2 = f32[16,512,2,240]{3,2,1,0:T(2,128)} fusion(f32[16,512,2,240]{3,2,1,0:T(2,128)} %get-tuple-element.192, pred[]{:T(512)S(6)} %compare.10, f32[512,2,240]{2,1,0:T(2,128)S(1)} %broadcast_select_fusion.2, f32[16,512]{1,0:T(8,128)S(1)} %dynamic-slice_bitcast_fusion.2), kind=kLoop, calls=%fused_computation.3.clone.1 | loop fusion | flops 11796480 | bytes 32473088 | tf_op jit(solution)/shard_map/while/body/eval_jaxpr/add | solution.py:53
  143.9 3.4 gather_fusion
  149.9 12.8 %select_add_fusion.2 = f32[16,512,2,240]{3,2,1,0:T(2,128)} fusion(f32[16,512,2,240]{3,2,1,0:T(2,128)} %get-tuple-element.192, pred[]{:T(512)S(6)} %compare.10, f32[512,2,240]{2,1,0:T(2,128)S(1)} %broadcast_select_fusion.2, f32[16,512]{1,0:T(8,128)S(1)} %dynamic-slice_bitcast_fusion.2), kind=kLoop, calls=%fused_computation.3.clone.1 | loop fusion | flops 11796480 | bytes 32473088 | tf_op jit(solution)/shard_map/while/body/eval_jaxpr/add | solution.py:53
  162.7 3.4 gather_fusion
  168.7 12.8 %select_add_fusion.2 = f32[16,512,2,240]{3,2,1,0:T(2,128)} fusion(f32[16,512,2,240]{3,2,1,0:T(2,128)} %get-tuple-element.192, pred[]{:T(512)S(6)} %compare.10, f32[512,2,240]{2,1,0:T(2,128)S(1)} %broadcast_select_fusion.2, f32[16,512]{1,0:T(8,128)S(1)} %dynamic-slice_bitcast_fusion.2), kind=kLoop, calls=%fused_computation.3.clone.1 | loop fusion | flops 11796480 | bytes 32473088 | tf_op jit(solution)/shard_map/while/body/eval_jaxpr/add | solution.py:53
  181.6 3.4 gather_fusion
  187.5 12.8 %select_add_fusion.2 = f32[16,512,2,240]{3,2,1,0:T(2,128)} fusion(f32[16,512,2,240]{3,2,1,0:T(2,128)} %get-tuple-element.192, pred[]{:T(512)S(6)} %compare.10, f32[512,2,240]{2,1,0:T(2,128)S(1)} %broadcast_select_fusion.2, f32[16,512]{1,0:T(8,128)S(1)} %dynamic-slice_bitcast_fusion.2), kind=kLoop, calls=%fused_computation.3.clone.1 | loop fusion | flops 11796480 | bytes 32473088 | tf_op jit(solution)/shard_map/while/body/eval_jaxpr/add | solution.py:53
  200.4 3.4 gather_fusion
  206.4 12.8 %select_add_fusion.2 = f32[16,512,2,240]{3,2,1,0:T(2,128)} fusion(f32[16,512,2,240]{3,2,1,0:T(2,128)} %get-tuple-element.192, pred[]{:T(512)S(6)} %compare.10, f32[512,2,240]{2,1,0:T(2,128)S(1)} %broadcast_select_fusion.2, f32[16,512]{1,0:T(8,128)S(1)} %dynamic-slice_bitcast_fusion.2), kind=kLoop, calls=%fused_computation.3.clone.1 | loop fusion | flops 11796480 | bytes 32473088 | tf_op jit(solution)/shard_map/while/body/eval_jaxpr/add | solution.py:53
  219.2 3.4 gather_fusion
  222.7 1.8 broadcast_select_fusion.2
  225.2 12.8 %select_add_fusion.2 = f32[16,512,2,240]{3,2,1,0:T(2,128)} fusion(f32[16,512,2,240]{3,2,1,0:T(2,128)} %get-tuple-element.192, pred[]{:T(512)S(6)} %compare.10, f32[512,2,240]{2,1,0:T(2,128)S(1)} %broadcast_select_fusion.2, f32[16,512]{1,0:T(8,128)S(1)} %dynamic-slice_bitcast_fusion.2), kind=kLoop, calls=%fused_computation.3.clone.1 | loop fusion | flops 11796480 | bytes 32473088 | tf_op jit(solution)/shard_map/while/body/eval_jaxpr/add | solution.py:53
  238.1 3.4 gather_fusion
  241.5 1.8 broadcast_select_fusion.2
  244.0 12.8 %select_add_fusion.2 = f32[16,512,2,240]{3,2,1,0:T(2,128)} fusion(f32[16,512,2,240]{3,2,1,0:T(2,128)} %get-tuple-element.192, pred[]{:T(512)S(6)} %compare.10, f32[512,2,240]{2,1,0:T(2,128)S(1)} %broadcast_select_fusion.2, f32[16,512]{1,0:T(8,128)S(1)} %dynamic-slice_bitcast_fusion.2), kind=kLoop, calls=%fused_computation.3.clone.1 | loop fusion | flops 11796480 | bytes 32473088 | tf_op jit(solution)/shard_map/while/body/eval_jaxpr/add | solution.py:53
  256.9 3.4 gather_fusion
  262.9 12.8 %select_add_fusion.2 = f32[16,512,2,240]{3,2,1,0:T(2,128)} fusion(f32[16,512,2,240]{3,2,1,0:T(2,128)} %get-tuple-element.192, pred[]{:T(512)S(6)} %compare.10, f32[512,2,240]{2,1,0:T(2,128)S(1)} %broadcast_select_fusion.2, f32[16,512]{1,0:T(8,128)S(1)} %dynamic-slice_bitcast_fusion.2), kind=kLoop, calls=%fused_computation.3.clone.1 | loop fusion | flops 11796480 | bytes 32473088 | tf_op jit(solution)/shard_map/while/body/eval_jaxpr/add | solution.py:53
  275.7 21.8 %fusion.7 = f32[2,60,512]{2,1,0:T(8,128)S(1)} fusion(f32[16,512,2,240]{3,2,1,0:T(2,128)} %get-tuple-element.99, f32[16,60,240]{2,0,1:T(8,128)S(1)} %copy-done.1), kind=kOutput, calls=%fused_computation.18 | convolution fusion | flops 2831155200 | bytes 16896000 | tf_op jit(solution)/shard_map/qrc,qakc->kra/dot_general | solution.py:58
  298.0 9.8 %all_gather.15 = f32[2,240,512]{2,0,1:T(2,128)S(1)} all-gather(f32[2,60,512]{2,0,1:T(2,128)S(1)} %copy.70), channel_id=1, replica_groups=mesh['freq'=2,'cell'=4,'sub'=4] {'sub'}, dimensions={1}, use_global_device_ids=true | all-gather | bytes 1228800 | tf_op jit(solution)/shard_map/all_gather | solution.py:88
  308.8 2.9 broadcast_in_dim.48
  311.6 47.5 %scatter_fusion = f32[2048,2,240]{2,1,0:T(2,128)} fusion(f32[2048,2,240]{2,1,0:T(2,128)} %broadcast_in_dim.48, s32[512]{0:T(512)S(1)} %bitcast.58, f32[512,2,240]{2,1,0:T(2,128)S(1)} %copy.71), kind=kCustom, calls=%fused_computation.2 | custom fusion | bytes 2951168 | tf_op jit(solution)/shard_map/scatter | solution.py:93
  359.1 7.2 %copy.73 = f32[4,4,128,2,240]{2,4,3,1,0:T(8,128)} copy(f32[4,4,128,2,240]{4,3,2,1,0:T(2,128)} %bitcast.50) | data formatting | bytes 7864320 | tf_op jit(solution)/shard_map/reshape | solution.py:95
  366.3 92.1 %all_to_all.10 = f32[4,4,128,2,240]{2,4,3,1,0:T(8,128)S(1)} all-to-all(f32[4,4,128,2,240]{2,4,3,1,0:T(8,128)} %copy.73), channel_id=1, replica_groups=mesh['freq'=2,'cell'=4,'sub'=4] {'cell'}, dimensions={0} | all-to-all | bytes 7864320 | tf_op jit(solution)/shard_map/all_to_all | solution.py:97
  458.4 2.7 fusion.4
  462.7 3.5 all-to-all-start.1
  466.2 24.0 %all-to-all-done.1 = f32[4,4,128,2,60]{2,1,4,3,0:T(4,128)S(1)} async-done(((f32[4,4,128,2,60]{2,1,4,3,0:T(4,128)}), f32[4,4,128,2,60]{2,1,4,3,0:T(4,128)S(1)}, u32[]{:S(2)}, u32[]{:S(2)}) %all-to-all-start.1) | async-done | bytes 983072 | tf_op jit(solution)/shard_map/all_to_all | solution.py:33
  491.4 2.1 gather_fusion.1
  493.7 1.8 bitcast_subtract_fusion
  (82 shorter events, 32.9 us)
Async XLA Ops:
  0.0 458.4 %copy-start = (f32[4,60,240]{2,0,1:T(4,128)S(1)}, f32[4,60,240]{2,0,1:T(4,128)}, u32[]{:S(2)}) copy-start(f32[4,60,240]{2,0,1:T(4,128)} %param.16) | copy-start | bytes 691204
  11.6 35.5 %collective-permute-start = (f32[128,2,240]{0,1,2:T(2,128)S(1)}, f32[128,2,240]{0,1,2:T(2,128)S(1)}, u32[]{:S(2)}, u32[]{:S(2)}) collective-permute-start(f32[128,2,240]{0,1,2:T(2,128)S(1)} %get-tuple-element.147), channel_id=1, source_target_pairs={{0,4},{4,8},{8,12},{1,5},{5,9},{9,13},{2,6},{6,10},{10,14},{3,7},{... | collective-permute-start | bytes 737288 | tf_op jit(solution)/shard_map/ppermute | solution.py:19
  15.1 32.0 %collective-permute-start.1 = (f32[128,2,240]{0,1,2:T(2,128)S(1)}, f32[128,2,240]{0,1,2:T(2,128)S(1)}, u32[]{:S(2)}, u32[]{:S(2)}) collective-permute-start(f32[128,2,240]{0,1,2:T(2,128)S(1)} %get-tuple-element.148), channel_id=1, source_target_pairs={{4,0},{8,4},{12,8},{5,1},{9,5},{13,9},{6,2},{10,6},{14,10},{7,3},{... | collective-permute-start | bytes 737288 | tf_op jit(solution)/shard_map/ppermute | solution.py:20
  50.7 225.0 %copy-start.1 = (f32[16,60,240]{2,0,1:T(8,128)S(1)}, f32[16,60,240]{2,0,1:T(8,128)}, u32[]{:S(2)}) copy-start(f32[16,60,240]{2,0,1:T(8,128)} %param.15) | copy-start | bytes 2764804
  462.7 27.5 %all-to-all-start.1 = ((f32[4,4,128,2,60]{2,1,4,3,0:T(4,128)}), f32[4,4,128,2,60]{2,1,4,3,0:T(4,128)S(1)}, u32[]{:S(2)}, u32[]{:S(2)}) async-start(f32[4,4,128,2,60]{2,1,4,3,0:T(4,128)} %copy.76), calls=%async_computation.1 | async-start | bytes 1966080 | tf_op jit(solution)/shard_map/all_to_all | solution.py:33
where the time goes:
time: 498 us; the launch traced here: 495 us
  other arithmetic  183 us (37%)
  blocking collectives  135 us (27%)
  local copies, waits for them, and re-layouts  117 us (23%)
  matrix products  27.6 us (6%)
  waiting for transfers between devices  24 us (5%)
  starting transfers between devices  8.3 us (2%)
    add x12, other arithmetic, add_pair(): return total + weights[step][:, :, None, None] * picked[None]  153 us
    all_to_all x1, blocking collectives, on_device(): lax.all_to_all(outgoing, 'cell', split_axis=0, concat_axis=0, tiled=True)  92.1 us
    scatter x1, local copies, waits for them, and re-layouts, on_device(): placed = jnp.zeros((cell_count * slots, nrhs_count, full_rows), jnp.float...  47.5 us
    gather x12, local copies, waits for them, and re-layouts, add_pair(): picked = jnp.take(extended, local_index[step], axis=0)  41 us
    all_to_all x1, waiting for transfers between devices, finish(): lax.all_to_all(total, 'cell', split_axis=0, concat_axis=0, tiled=True)  24 us
    dot_general x1, matrix products, on_device(): near = jnp.einsum('qrc,qakc->kra', translation, mixed, precision=highest)  21.8 us
    select_n x24, other arithmetic, add_pair(): picked = jnp.take(extended, local_index[step], axis=0)  21.4 us
    all_gather x1, blocking collectives, on_device(): all_sums = lax.all_gather(box_sums, 'cell', axis=2, tiled=True)  15.9 us
  transfers between devices with their start and end apart: 3, of which 1 were waited for; matrix products, arithmetic and copies ran while one was open for 2% of the time, Pallas kernels for 0%

commit v1 on v0

v1 whole, which is shorter than its diff:
```python
import functools

import jax
import jax.numpy as jnp
from jax import lax
from jax.experimental import pallas as pl
from jax.experimental.pallas import tpu as pltpu
from jax.sharding import PartitionSpec as P

BOX_DEV = 16
WIN = 128
BLK = 128
MESH = pl.DeviceIdType.MESH
F32 = jnp.float32
BF16 = jnp.bfloat16
HIGHEST = lax.Precision.HIGHEST


def split(x):
    high = x.astype(BF16)
    return high, (x - high.astype(F32)).astype(BF16)


def dot3(ah, al, bh, bl):
    dot = functools.partial(jnp.dot, preferred_element_type=F32)
    return dot(ah, bh) + (dot(ah, bl) + dot(al, bh))


def kernel(
    cells, subs,
    dir_ref, nbr_ref, spc_ref, kind_ref, box_ref, t_ref, r_ref, cm_ref, out_ref,
    ext, gown, gall, rsend, rall, inc, wts, nls, w2, y2, tpad, dfull, dh, dl, rh, rl, ffull,
    dir_send, dir_recv, halo_send, halo_recv, r_send, r_recv, g_send, g_recv, inc_send, inc_recv,
):
    nrhs, rows, atoms = dir_ref.shape
    nb, terms = nbr_ref.shape[0], t_ref.shape[0]
    types, full = r_ref.shape[0], r_ref.shape[2]
    blocks = atoms // BLK
    span = BLK + 2 * WIN
    pad = 64
    cell, sub = lax.axis_index("cell"), lax.axis_index("sub")
    has_left, has_right = cell > 0, cell < cells - 1

    def copy(src, dst, send, recv, to_cell, to_sub):
        return pltpu.make_async_remote_copy(
            src_ref=src, dst_ref=dst, send_sem=send, recv_sem=recv,
            device_id={"cell": to_cell, "sub": to_sub}, device_id_type=MESH,
        )

    def each_far_cell(body):
        def step(other, carry):
            @pl.when(other != cell)
            def _():
                body(other)
            return carry
        lax.fori_loop(0, cells, step, 0)

    barrier = pltpu.get_barrier_semaphore()

    def greet(to_cell, to_sub):
        pl.semaphore_signal(
            barrier, inc=1, device_id={"cell": to_cell, "sub": to_sub}, device_id_type=MESH
        )

    for d in range(1, subs):
        greet(cell, lax.rem(sub + d, subs))
    for present, other in ((has_left, cell - 1), (has_right, cell + 1)):
        @pl.when(present)
        def _():
            for d in range(1, subs):
                greet(other, lax.rem(sub + d, subs))
    each_far_cell(lambda other: greet(other, sub))
    sides = has_left.astype(jnp.int32) + has_right.astype(jnp.int32)
    pl.semaphore_wait(barrier, (subs - 1) * (1 + sides) + cells - 1)

    def dir_copy(d):
        return copy(
            dir_ref, ext.at[sub, :, :, pl.ds(WIN, atoms)], dir_send.at[d], dir_recv.at[sub],
            cell, lax.rem(sub + d, subs),
        )

    def halo_copy(side, d):
        start = atoms - WIN if side == 0 else 0
        place = 0 if side == 0 else WIN + atoms
        other = cell + 1 if side == 0 else cell - 1
        return copy(
            dir_ref.at[:, :, pl.ds(start, WIN)], ext.at[sub, :, :, pl.ds(place, WIN)],
            halo_send.at[side, d], halo_recv.at[side, sub], other, lax.rem(sub + d, subs),
        )

    def r_copy(other):
        return copy(rsend, rall.at[cell], r_send.at[other], r_recv.at[cell], other, sub)

    def g_copy(other):
        return copy(gown, gall.at[cell], g_send.at[other], g_recv.at[cell], other, sub)

    def inc_copy(b, d):
        return copy(
            inc.at[sub, b], inc.at[sub, b], inc_send.at[b, d], inc_recv.at[b, sub],
            cell, lax.rem(sub + d, subs),
        )

    for d in range(1, subs):
        dir_copy(d).start()
    for side, present in ((0, has_right), (1, has_left)):
        @pl.when(present)
        def _():
            for d in range(subs):
                halo_copy(side, d).start()
    for side, present in ((0, has_left), (1, has_right)):
        @pl.when(jnp.logical_not(present))
        def _():
            place = 0 if side == 0 else WIN + atoms
            ext[:, :, :, pl.ds(place, WIN)] = jnp.zeros((subs, nrhs, rows, WIN), F32)
    ext[sub, :, :, pl.ds(WIN, atoms)] = dir_ref[...]

    rsend[...] = jnp.zeros_like(rsend)
    for t in range(types):
        rsend[t * pad:t * pad + rows, :] = r_ref[t]
    each_far_cell(lambda other: r_copy(other).start())
    rall[cell] = rsend[...]

    orders = lax.broadcasted_iota(jnp.int32, (terms, 1), 0).astype(F32)
    wide = nbr_ref[...] - (cell * atoms - WIN)
    near_rows = [wide[n:n + 1] for n in range(nb)]
    plain = []
    for n in range(nb):
        s = spc_ref[n:n + 1, :]
        plain.append(jnp.cos(0.9 * orders * s) / s)
    dead = [None] * nb
    for n in range(nb):
        total = plain[n]
        for m in range(n + 1, nb):
            same = near_rows[n] == near_rows[m]
            total = total + jnp.where(same, plain[m], 0.0)
            flag = same.astype(jnp.int32)
            dead[m] = flag if dead[m] is None else dead[m] | flag
        wts[n] = total
        row = near_rows[n]
        if dead[n] is not None:
            row = jnp.where(dead[n] > 0, -1, row)
        nls[n:n + 1, :] = row

    chunk, group = 32, 8
    for b in range(blocks):
        lanes = slice(b * BLK, (b + 1) * BLK)

        def spread(step, carry):
            base = lax.broadcasted_iota(jnp.int32, (chunk, BLK), 0) + (b * BLK + step * chunk)
            for q0 in range(0, terms, group):
                acc = [jnp.zeros((chunk, BLK), F32)] * group
                for n in range(nb):
                    hit = nls[n:n + 1, lanes] == base
                    for q in range(group):
                        acc[q] = jnp.where(hit, wts[n, q0 + q:q0 + q + 1, lanes], acc[q])
                for q in range(group):
                    high, low = split(acc[q])
                    place = pl.ds(pl.multiple_of((q0 + q) * span + step * chunk, chunk), chunk)
                    w2[b, place, 0:BLK] = high
                    w2[b, place, BLK:2 * BLK] = low
            return carry

        lax.fori_loop(0, span // chunk, spread, 0)

    tpad[...] = jnp.zeros_like(tpad)
    for q in range(terms):
        tpad[q * pad:q * pad + rows, :] = t_ref[q]

    for d in range(1, subs):
        other = lax.rem(sub + d, subs)
        piece = ext.at[other, :, :, pl.ds(WIN, atoms)]
        copy(piece, piece, dir_send.at[d], dir_recv.at[other], cell, other).wait_recv()
    for s in range(subs):
        for k in range(nrhs):
            dfull[k, s * rows:(s + 1) * rows, WIN:WIN + atoms] = ext[s, k, :, WIN:WIN + atoms]

    first_box = cell * BOX_DEV
    box_ids = lax.broadcasted_iota(jnp.int32, (BOX_DEV, 1), 0) + first_box
    member = (box_ref[...] == box_ids).astype(F32)
    member_h = member.astype(BF16)
    gown[...] = jnp.zeros_like(gown)
    nt = (((1,), (1,)), ((), ()))
    for k in range(nrhs):
        ch, cl = split(dfull[k, :, WIN:WIN + atoms])
        dh[k, :, WIN:WIN + atoms] = ch
        dl[k, :, WIN:WIN + atoms] = cl
        sums = lax.dot_general(ch, member_h, nt, preferred_element_type=F32) + lax.dot_general(
            cl, member_h, nt, preferred_element_type=F32
        )
        gown[k * pad:k * pad + rows, :] = jnp.dot(
            cm_ref[...], sums, precision=HIGHEST, preferred_element_type=F32
        )
    each_far_cell(lambda other: g_copy(other).start())
    gall[cell] = gown[...]

    for side, present in ((0, has_left), (1, has_right)):
        @pl.when(present)
        def _():
            place = 0 if side == 0 else WIN + atoms
            for s in range(subs):
                piece = ext.at[s, :, :, pl.ds(place, WIN)]
                copy(
                    piece, piece, halo_send.at[side, s], halo_recv.at[side, s], cell, s
                ).wait_recv()
    for place in (0, WIN + atoms):
        lanes = slice(place, place + WIN)
        for k in range(nrhs):
            for s in range(subs):
                dfull[k, s * rows:(s + 1) * rows, lanes] = ext[s, k, :, lanes]
            high, low = split(dfull[k, :, lanes])
            dh[k, :, lanes] = high
            dl[k, :, lanes] = low

    per = 4
    for q0 in range(0, terms, per):
        th, tl = split(tpad[q0 * pad:(q0 + per) * pad, :])
        for k in range(nrhs):
            high, low = split(dot3(th, tl, dh[k], dl[k]))
            for q in range(per):
                y2[q0 + q, k * pad:(k + 1) * pad, :] = high[q * pad:(q + 1) * pad]
                y2[q0 + q, (nrhs + k) * pad:(nrhs + k + 1) * pad, :] = low[q * pad:(q + 1) * pad]

    def wait_g(other):
        copy(gown, gall.at[other], g_send.at[other], g_recv.at[other], other, sub).wait_recv()

    each_far_cell(wait_g)
    far_box = jnp.zeros((nrhs * pad, BOX_DEV), F32)
    row_id = lax.broadcasted_iota(jnp.int32, (BOX_DEV, BOX_DEV), 0)
    col_id = lax.broadcasted_iota(jnp.int32, (BOX_DEV, BOX_DEV), 1)
    for c in range(cells):
        offsets = ((row_id + c * BOX_DEV) - (col_id + first_box)).astype(F32)
        green = jnp.where(
            offsets == 0.0, 0.0,
            jnp.cos(1.3 * offsets) / jnp.sqrt(jnp.maximum(jnp.abs(offsets), 1.0)),
        )
        far_box += jnp.dot(gall[c], green, precision=HIGHEST, preferred_element_type=F32)
    fbh, fbl = split(far_box)

    half = nrhs * pad
    for b in range(blocks):
        window = slice(b * BLK, b * BLK + span)
        left = jnp.concatenate([y2[q, :, window] for q in range(terms)], axis=1)
        prod = jnp.dot(left, w2[b], preferred_element_type=F32)
        near = (prod[:half, :BLK] + (prod[:half, BLK:] + prod[half:, :BLK])) + prod[half:, BLK:]
        mb = member_h[:, b * BLK:(b + 1) * BLK]
        far = jnp.dot(fbh, mb, preferred_element_type=F32) + jnp.dot(
            fbl, mb, preferred_element_type=F32
        )
        inc[sub, b] = near + far
        for d in range(1, subs):
            inc_copy(b, d).start()

    def wait_r(other):
        copy(rsend, rall.at[other], r_send.at[other], r_recv.at[other], other, sub).wait_recv()

    each_far_cell(wait_r)

    def split_r(c, carry):
        rh[c], rl[c] = split(rall[c])
        return carry

    lax.fori_loop(0, cells, split_r, 0)

    for b in range(blocks):
        lanes = slice(b * BLK, (b + 1) * BLK)
        for d in range(1, subs):
            other = lax.rem(sub + d, subs)
            piece = inc.at[other, b]
            copy(piece, piece, inc_send.at[b, d], inc_recv.at[b, other], cell, other).wait_recv()
        for s in range(subs):
            for k in range(nrhs):
                ffull[s * rows:(s + 1) * rows, k * BLK:(k + 1) * BLK] = inc[
                    s, b, k * pad:k * pad + rows, :
                ]
        fh, fl = split(ffull[...])
        kinds = kind_ref[:, lanes]
        kinds = jnp.concatenate([kinds] * nrhs, axis=1)

        def apply(c, total):
            prod = dot3(rh[c], rl[c], fh, fl)
            for t in range(types):
                total = jnp.where(kinds == c * types + t, prod[t * pad:(t + 1) * pad], total)
            return total

        total = jnp.zeros((pad, nrhs * BLK), F32)
        if cells <= 4:
            for c in range(cells):
                total = apply(c, total)
        else:
            total = lax.fori_loop(0, cells, apply, total)
        for k in range(nrhs):
            out_ref[k, :, lanes] = dir_ref[k, :, lanes] - total[:rows, k * BLK:(k + 1) * BLK]

    for d in range(1, subs):
        dir_copy(d).wait_send()
        for b in range(blocks):
            inc_copy(b, d).wait_send()
    for side, present in ((0, has_right), (1, has_left)):
        @pl.when(present)
        def _():
            for d in range(subs):
                halo_copy(side, d).wait_send()

    def sent(other):
        r_copy(other).wait_send()
        g_copy(other).wait_send()

    each_far_cell(sent)


def on_device(
    cells, subs,
    direction, neighbours, spacing, scatterer, box_index, translation, response, coarse_map
):
    nrhs, rows, atoms = direction.shape
    nb = neighbours.shape[0]
    terms, _, full = translation.shape
    types = response.shape[0]
    blocks = atoms // BLK
    span, reach, pad = BLK + 2 * WIN, atoms + 2 * WIN, 64
    dma = pltpu.SemaphoreType.DMA
    return pl.pallas_call(
        functools.partial(kernel, cells, subs),
        out_shape=jax.ShapeDtypeStruct(direction.shape, F32),
        in_specs=[pl.BlockSpec(memory_space=pltpu.VMEM)] * 8,
        out_specs=pl.BlockSpec(memory_space=pltpu.VMEM),
        scratch_shapes=[
            pltpu.VMEM((subs, nrhs, rows, reach), F32),
            pltpu.VMEM((nrhs * pad, BOX_DEV), F32),
            pltpu.VMEM((cells, nrhs * pad, BOX_DEV), F32),
            pltpu.VMEM((types * pad, full), F32),
            pltpu.VMEM((cells, types * pad, full), F32),
            pltpu.VMEM((subs, blocks, nrhs * pad, BLK), F32),
            pltpu.VMEM((nb, terms, atoms), F32),
            pltpu.VMEM((nb, atoms), jnp.int32),
            pltpu.VMEM((blocks, terms * span, 2 * BLK), BF16),
            pltpu.VMEM((terms, 2 * nrhs * pad, reach), BF16),
            pltpu.VMEM((terms * pad, full), F32),
            pltpu.VMEM((nrhs, full, reach), F32),
            pltpu.VMEM((nrhs, full, reach), BF16),
            pltpu.VMEM((nrhs, full, reach), BF16),
            pltpu.VMEM((cells, types * pad, full), BF16),
            pltpu.VMEM((cells, types * pad, full), BF16),
            pltpu.VMEM((full, nrhs * BLK), F32),
            dma((subs,)), dma((subs,)), dma((2, subs)), dma((2, subs)),
            dma((cells,)), dma((cells,)), dma((cells,)), dma((cells,)),
            dma((blocks, subs)), dma((blocks, subs)),
        ],
        compiler_params=pltpu.CompilerParams(
            collective_id=0, has_side_effects=True, vmem_limit_bytes=56 * 1024 * 1024
        ),
    )(
        direction, neighbours, spacing, scatterer.reshape(1, atoms), box_index.reshape(1, atoms),
        translation, response, coarse_map,
    )


def solution(mesh):
    in_specs = (
        P("freq", "sub", "cell"),
        P(None, "cell"),
        P(None, "cell"),
        P("cell", None),
        P("cell"),
        P(None, "sub", "freq"),
        P("cell", "sub", "freq"),
        P("sub", "freq"),
    )
    out_specs = P("freq", "sub", "cell")
    return jax.shard_map(
        functools.partial(on_device, mesh.shape["cell"], mesh.shape["sub"]),
        mesh=mesh, in_specs=in_specs, out_specs=out_specs, check_vma=False,
    )
```

time: 498 us -> 64 us (0.13)
  other arithmetic: 183 us -> 0 us
  blocking collectives: 135 us -> 0 us
  local copies, waits for them, and re-layouts: 117 us -> 6.89 us
  Pallas kernels: 0 us -> 56.8 us
  matrix products: 27.6 us -> 0 us
  waiting for transfers between devices: 24 us -> 0 us
  starting transfers between devices: 8.3 us -> 0 us
    add x13 -> x0, other arithmetic: 153 us -> none  [the longest x12 153 us: add_pair(): return total + weights[step][:, :, None, None] * picked[None]]
    all_to_all x1 -> x0, blocking collectives: 92.1 us -> none  [on_device(): lax.all_to_all(outgoing, 'cell', split_axis=0, concat_axis=0, tiled=True)]
    pallas_call x0 -> x1, Pallas kernels: none -> 56.8 us  [on_device(): pl.pallas_call(functools.partial(kernel, cells, subs), out_shape=jax.Shap...]
    scatter x1 -> x0, local copies, waits for them, and re-layouts: 47.5 us -> none  [on_device(): placed = jnp.zeros((cell_count * slots, nrhs_count, full_rows), jnp.float...]
    gather x14 -> x0, local copies, waits for them, and re-layouts: 43.3 us -> none  [the longest x12 41 us: add_pair(): picked = jnp.take(extended, local_index[step], axis=0)]
    all_gather x4 -> x0, blocking collectives: 42.8 us -> none  [the longest x1 15.9 us: on_device(): all_sums = lax.all_gather(box_sums, 'cell', axis=2, tiled=True)]
    dot_general x6 -> x0, matrix products: 27.6 us -> none  [the longest x1 21.8 us: on_device(): near = jnp.einsum('qrc,qakc->kra', translation, mixed, precision=highest)]
    all_to_all x1 -> x0, waiting for transfers between devices: 24 us -> none  [finish(): lax.all_to_all(total, 'cell', split_axis=0, concat_axis=0, tiled=True)]
  transfers between devices with their start and end apart: 3 -> 0, of which waited for: 1 -> 0; matrix products, arithmetic and copies ran while one was open for 2% -> 0% of each run, Pallas kernels for 0% -> 0%
where the time goes in v1:
time: 64 us; the launch traced here: 63.7 us
  Pallas kernels  56.8 us (89%)
  local copies, waits for them, and re-layouts  6.89 us (11%)
    pallas_call x1, Pallas kernels, on_device(): pl.pallas_call(functools.partial(kernel, cells, subs), out_shape=jax.Shap...  56.8 us
    unnamed x5, local copies, waits for them, and re-layouts  5.06 us
    pallas_call x1, local copies, waits for them, and re-layouts, on_device(): pl.pallas_call(functools.partial(kernel, cells, subs), out_shape=jax.Shap...  1.83 us

profile of v1, /device:TPU:0, one launch (start us, length us, event | category | flops | bytes accessed | tf_op | source)
XLA Modules:
  0.0 63.7 jit_solution(17127213622203246674)
XLA Ops:
  0.0 0.0 copy-start
  0.0 1.8 %copy.9.dir_ref = f32[2,60,512]{2,1,0:T(8,128)} copy(f32[2,60,512]{2,0,1:T(2,128)} %param.8) | data formatting | bytes 491520 | tf_op args[0]
  1.8 1.7 %copy.11.r_ref = f32[4,60,240]{2,1,0:T(8,128)} copy(f32[4,60,240]{2,0,1:T(4,128)} %param.14) | data formatting | bytes 460800 | tf_op args[6]
  3.5 0.0 copy-done
  3.5 1.6 %copy.10.t_ref = f32[16,60,240]{2,1,0:T(8,128)} copy(f32[16,60,240]{2,0,1:T(8,128)S(1)} %copy-done) | data formatting | bytes 1843200 | tf_op args[5]
  5.1 56.8 %shard_map.82 = f32[2,60,512]{2,1,0:T(8,128)} custom-call(f32[2,60,512]{2,1,0:T(8,128)} %copy.9.dir_ref, s32[12,512]{1,0:T(8,128)} %nbr_ref.1, f32[12,512]{1,0:T(8,128)} %spc_ref.1, s32[1,512]{1,0:T(1,128)} %bitcast.2, s32[1,512]{1,0:T(1,128)} %bitcast.3, f32[16,60,240]{2,1,0:T(8,128)} %copy.10.t_ref, f32[4,60,240]{2,1,0:T(8,128)} %copy.11.r_ref, ...), custom_call_target="tpu_custom_call" | custom-call | tf_op jit(solution)/shard_map/pallas_call | solution.py:322
  61.9 1.8 %copy.12 = f32[2,60,512]{2,0,1:T(2,128)} copy(f32[2,60,512]{2,1,0:T(8,128)} %shard_map.82) | data formatting | bytes 491520 | tf_op jit(solution)/shard_map/pallas_call | solution.py:322
Async XLA Ops:
  0.0 3.5 %copy-start = (f32[16,60,240]{2,0,1:T(8,128)S(1)}, f32[16,60,240]{2,0,1:T(8,128)}, u32[]{:S(2)}) copy-start(f32[16,60,240]{2,0,1:T(8,128)} %param.13) | copy-start | bytes 2764804

commit v2 on v1

--- a/solution.py
+++ b/solution.py
@@ -29,7 +29,7 @@
 def kernel(
     cells, subs,
     dir_ref, nbr_ref, spc_ref, kind_ref, box_ref, t_ref, r_ref, cm_ref, out_ref,
-    ext, gown, gall, rsend, rall, inc, wts, nls, w2, y2, tpad, dfull, dh, dl, rh, rl, ffull,
+    ext, gown, gall, rall, inc, wts, nls, w2, y2, tpad, dfull, dh, dl, rh, rl, ffull,
     dir_send, dir_recv, halo_send, halo_recv, r_send, r_recv, g_send, g_recv, inc_send, inc_recv,
 ):
     nrhs, rows, atoms = dir_ref.shape
@@ -62,51 +62,71 @@
             barrier, inc=1, device_id={"cell": to_cell, "sub": to_sub}, device_id_type=MESH
         )
 
-    for d in range(1, subs):
-        greet(cell, lax.rem(sub + d, subs))
-    for present, other in ((has_left, cell - 1), (has_right, cell + 1)):
-        @pl.when(present)
-        def _():
-            for d in range(1, subs):
-                greet(other, lax.rem(sub + d, subs))
+    mate, peer = sub + 1 - 2 * lax.rem(sub, 2), lax.rem(sub + 2, subs)
+    cross = lax.rem(mate + 2, subs)
+    greet(cell, mate)
+    greet(cell, peer)
     each_far_cell(lambda other: greet(other, sub))
-    sides = has_left.astype(jnp.int32) + has_right.astype(jnp.int32)
-    pl.semaphore_wait(barrier, (subs - 1) * (1 + sides) + cells - 1)
-
-    def dir_copy(d):
+    pl.semaphore_wait(barrier, cells + 1)
+
+    parts = (pl.ds(0, WIN), pl.ds(WIN, atoms), pl.ds(WIN + atoms, WIN))
+    parts_there = ((0, has_left), (2, has_right))
+
+    def rows_copy(part, way, origin, src=None):
+        piece = ext.at[origin, :, :, parts[part]]
+        to = peer if way == 1 else mate
         return copy(
-            dir_ref, ext.at[sub, :, :, pl.ds(WIN, atoms)], dir_send.at[d], dir_recv.at[sub],
-            cell, lax.rem(sub + d, subs),
-        )
-
-    def halo_copy(side, d):
+            piece if src is None else src, piece, dir_send.at[part, way],
+            dir_recv.at[part, origin], cell, to,
+        )
+
+    def relay(part):
+        rows_copy(part, 2, peer).wait_recv()
+        rows_copy(part, 2, peer).start()
+
+    def halo_copy(side):
         start = atoms - WIN if side == 0 else 0
-        place = 0 if side == 0 else WIN + atoms
         other = cell + 1 if side == 0 else cell - 1
         return copy(
-            dir_ref.at[:, :, pl.ds(start, WIN)], ext.at[sub, :, :, pl.ds(place, WIN)],
-            halo_send.at[side, d], halo_recv.at[side, sub], other, lax.rem(sub + d, subs),
-        )
-
-    def r_copy(other):
-        return copy(rsend, rall.at[cell], r_send.at[other], r_recv.at[cell], other, sub)
+            dir_ref.at[:, :, pl.ds(start, WIN)], ext.at[sub, :, :, parts[2 * side]],
+            halo_send.at[side], halo_recv.at[side], other, sub,
+        )
+
+    def r_copy(way, shard):
+        other = cell + 1 if way == 0 else cell - 1
+        piece = rall.at[shard]
+        return copy(piece, piece, r_send.at[way, shard], r_recv.at[shard], other, sub)
+
+    def hop(h):
+        for way, shard, inside, onward in (
+            (0, cell - h, cell - h >= 0, has_right), (1, cell + h, cell + h < cells, has_left)
+        ):
+            @pl.when(inside)
+            def _():
+                r_copy(way, shard).wait_recv()
+
+            @pl.when(jnp.logical_and(inside, onward))
+            def _():
+                r_copy(way, shard).start()
 
     def g_copy(other):
         return copy(gown, gall.at[cell], g_send.at[other], g_recv.at[cell], other, sub)
 
-    def inc_copy(b, d):
-        return copy(
-            inc.at[sub, b], inc.at[sub, b], inc_send.at[b, d], inc_recv.at[b, sub],
-            cell, lax.rem(sub + d, subs),
-        )
-
-    for d in range(1, subs):
-        dir_copy(d).start()
+    def inc_copy(b, way, origin):
+        piece = inc.at[origin, b]
+        to = peer if way == 1 else mate
+        return copy(piece, piece, inc_send.at[b, way], inc_recv.at[b, origin], cell, to)
+
+    def inc_relay(b):
+        inc_copy(b, 2, peer).wait_recv()
+        inc_copy(b, 2, peer).start()
+
     for side, present in ((0, has_right), (1, has_left)):
         @pl.when(present)
         def _():
-            for d in range(subs):
-                halo_copy(side, d).start()
+            halo_copy(side).start()
+    for way in (1, 0):
+        rows_copy(1, way, sub, dir_ref).start()
     for side, present in ((0, has_left), (1, has_right)):
         @pl.when(jnp.logical_not(present))
         def _():
@@ -114,11 +134,13 @@
             ext[:, :, :, pl.ds(place, WIN)] = jnp.zeros((subs, nrhs, rows, WIN), F32)
     ext[sub, :, :, pl.ds(WIN, atoms)] = dir_ref[...]
 
-    rsend[...] = jnp.zeros_like(rsend)
+    rall[cell] = jnp.zeros((types * pad, full), F32)
     for t in range(types):
-        rsend[t * pad:t * pad + rows, :] = r_ref[t]
-    each_far_cell(lambda other: r_copy(other).start())
-    rall[cell] = rsend[...]
+        rall[cell, t * pad:t * pad + rows, :] = r_ref[t]
+    for way, present in ((0, has_right), (1, has_left)):
+        @pl.when(present)
+        def _():
+            r_copy(way, cell).start()
 
     orders = lax.broadcasted_iota(jnp.int32, (terms, 1), 0).astype(F32)
     wide = nbr_ref[...] - (cell * atoms - WIN)
@@ -161,15 +183,27 @@
             return carry
 
         lax.fori_loop(0, span // chunk, spread, 0)
+        if b == 0:
+            for part, present in parts_there:
+                @pl.when(present)
+                def _():
+                    halo_copy(part // 2).wait_recv()
+                    for way in (1, 0):
+                        rows_copy(part, way, sub).start()
+        if b == blocks // 2:
+            relay(1)
 
     tpad[...] = jnp.zeros_like(tpad)
     for q in range(terms):
         tpad[q * pad:q * pad + rows, :] = t_ref[q]
 
-    for d in range(1, subs):
-        other = lax.rem(sub + d, subs)
-        piece = ext.at[other, :, :, pl.ds(WIN, atoms)]
-        copy(piece, piece, dir_send.at[d], dir_recv.at[other], cell, other).wait_recv()
+    for part, present in parts_there:
+        @pl.when(present)
+        def _():
+            relay(part)
+    hop(1)
+    for origin in (mate, cross):
+        rows_copy(1, 0, origin).wait_recv()
     for s in range(subs):
         for k in range(nrhs):
             dfull[k, s * rows:(s + 1) * rows, WIN:WIN + atoms] = ext[s, k, :, WIN:WIN + atoms]
@@ -193,15 +227,11 @@
     each_far_cell(lambda other: g_copy(other).start())
     gall[cell] = gown[...]
 
-    for side, present in ((0, has_left), (1, has_right)):
+    for part, present in parts_there:
         @pl.when(present)
         def _():
-            place = 0 if side == 0 else WIN + atoms
-            for s in range(subs):
-                piece = ext.at[s, :, :, pl.ds(place, WIN)]
-                copy(
-                    piece, piece, halo_send.at[side, s], halo_recv.at[side, s], cell, s
-                ).wait_recv()
+            for origin in (mate, cross):
+                rows_copy(part, 0, origin).wait_recv()
     for place in (0, WIN + atoms):
         lanes = slice(place, place + WIN)
         for k in range(nrhs):
@@ -219,6 +249,9 @@
             for q in range(per):
                 y2[q0 + q, k * pad:(k + 1) * pad, :] = high[q * pad:(q + 1) * pad]
                 y2[q0 + q, (nrhs + k) * pad:(nrhs + k + 1) * pad, :] = low[q * pad:(q + 1) * pad]
+
+    if cells > 2:
+        hop(2)
 
     def wait_g(other):
         copy(gown, gall.at[other], g_send.at[other], g_recv.at[other], other, sub).wait_recv()
@@ -247,13 +280,16 @@
             fbl, mb, preferred_element_type=F32
         )
         inc[sub, b] = near + far
-        for d in range(1, subs):
-            inc_copy(b, d).start()
-
-    def wait_r(other):
-        copy(rsend, rall.at[other], r_send.at[other], r_recv.at[other], other, sub).wait_recv()
-
-    each_far_cell(wait_r)
+        for way in (1, 0):
+            inc_copy(b, way, sub).start()
+        if b >= 2:
+            inc_relay(b - 2)
+
+    def last_hops(h, carry):
+        hop(h)
+        return carry
+
+    lax.fori_loop(3, cells, last_hops, 0)
 
     def split_r(c, carry):
         rh[c], rl[c] = split(rall[c])
@@ -263,10 +299,10 @@
 
     for b in range(blocks):
         lanes = slice(b * BLK, (b + 1) * BLK)
-        for d in range(1, subs):
-            other = lax.rem(sub + d, subs)
-            piece = inc.at[other, b]
-            copy(piece, piece, inc_send.at[b, d], inc_recv.at[b, other], cell, other).wait_recv()
+        if b + max(blocks - 2, 0) < blocks:
+            inc_relay(b + max(blocks - 2, 0))
+        for origin in (mate, cross):
+            inc_copy(b, 0, origin).wait_recv()
         for s in range(subs):
             for k in range(nrhs):
                 ffull[s * rows:(s + 1) * rows, k * BLK:(k + 1) * BLK] = inc[
@@ -291,21 +327,31 @@
         for k in range(nrhs):
             out_ref[k, :, lanes] = dir_ref[k, :, lanes] - total[:rows, k * BLK:(k + 1) * BLK]
 
-    for d in range(1, subs):
-        dir_copy(d).wait_send()
+    for way in range(3):
+        rows_copy(1, way, sub).wait_send()
         for b in range(blocks):
-            inc_copy(b, d).wait_send()
+            inc_copy(b, way, sub).wait_send()
+        for part, present in parts_there:
+            @pl.when(present)
+            def _():
+                rows_copy(part, way, sub).wait_send()
     for side, present in ((0, has_right), (1, has_left)):
         @pl.when(present)
         def _():
-            for d in range(subs):
-                halo_copy(side, d).wait_send()
-
-    def sent(other):
-        r_copy(other).wait_send()
-        g_copy(other).wait_send()
-
-    each_far_cell(sent)
+            halo_copy(side).wait_send()
+
+    def sent(shard, carry):
+        for way, goes in (
+            (0, jnp.logical_and(shard <= cell, has_right)),
+            (1, jnp.logical_and(shard >= cell, has_left)),
+        ):
+            @pl.when(goes)
+            def _():
+                r_copy(way, shard).wait_send()
+        return carry
+
+    lax.fori_loop(0, cells, sent, 0)
+    each_far_cell(lambda other: g_copy(other).wait_send())
 
 
 def on_device(
@@ -328,7 +374,6 @@
             pltpu.VMEM((subs, nrhs, rows, reach), F32),
             pltpu.VMEM((nrhs * pad, BOX_DEV), F32),
             pltpu.VMEM((cells, nrhs * pad, BOX_DEV), F32),
-            pltpu.VMEM((types * pad, full), F32),
             pltpu.VMEM((cells, types * pad, full), F32),
             pltpu.VMEM((subs, blocks, nrhs * pad, BLK), F32),
             pltpu.VMEM((nb, terms, atoms), F32),
@@ -342,9 +387,9 @@
             pltpu.VMEM((cells, types * pad, full), BF16),
             pltpu.VMEM((cells, types * pad, full), BF16),
             pltpu.VMEM((full, nrhs * BLK), F32),
-            dma((subs,)), dma((subs,)), dma((2, subs)), dma((2, subs)),
-            dma((cells,)), dma((cells,)), dma((cells,)), dma((cells,)),
-            dma((blocks, subs)), dma((blocks, subs)),
+            dma((3, 3)), dma((3, subs)), dma((2,)), dma((2,)),
+            dma((2, cells)), dma((cells,)), dma((cells,)), dma((cells,)),
+            dma((blocks, 3)), dma((blocks, subs)),
         ],
         compiler_params=pltpu.CompilerParams(
             collective_id=0, has_side_effects=True, vmem_limit_bytes=56 * 1024 * 1024

time: 64 us -> 51.2 us (0.80)
  Pallas kernels: 56.8 us -> 44.1 us
    pallas_call x1, Pallas kernels: 56.8 us -> 44.1 us  [on_device(): pl.pallas_call(functools.partial(kernel, cells, subs), out_shape=jax.Shap...]
where the time goes in v2:
time: 51.2 us; the launch traced here: 51 us
  Pallas kernels  44.1 us (86%)
  local copies, waits for them, and re-layouts  6.89 us (13%)
    pallas_call x1, Pallas kernels, on_device(): pl.pallas_call(functools.partial(kernel, cells, subs), out_shape=jax.Shap...  44.1 us
    unnamed x5, local copies, waits for them, and re-layouts  5.06 us
    pallas_call x1, local copies, waits for them, and re-layouts, on_device(): pl.pallas_call(functools.partial(kernel, cells, subs), out_shape=jax.Shap...  1.83 us

profile of v2, /device:TPU:0, one launch (start us, length us, event | category | flops | bytes accessed | tf_op | source)
XLA Modules:
  0.0 51.0 jit_solution(3447536841646170715)
XLA Ops:
  0.0 0.0 copy-start
  0.0 1.8 %copy.9.dir_ref = f32[2,60,512]{2,1,0:T(8,128)} copy(f32[2,60,512]{2,0,1:T(2,128)} %param.8) | data formatting | bytes 491520 | tf_op args[0]
  1.8 1.7 %copy.11.r_ref = f32[4,60,240]{2,1,0:T(8,128)} copy(f32[4,60,240]{2,0,1:T(4,128)} %param.14) | data formatting | bytes 460800 | tf_op args[6]
  3.5 0.0 copy-done
  3.5 1.6 %copy.10.t_ref = f32[16,60,240]{2,1,0:T(8,128)} copy(f32[16,60,240]{2,0,1:T(8,128)S(1)} %copy-done) | data formatting | bytes 1843200 | tf_op args[5]
  5.1 44.1 %shard_map.82 = f32[2,60,512]{2,1,0:T(8,128)} custom-call(f32[2,60,512]{2,1,0:T(8,128)} %copy.9.dir_ref, s32[12,512]{1,0:T(8,128)} %nbr_ref.1, f32[12,512]{1,0:T(8,128)} %spc_ref.1, s32[1,512]{1,0:T(1,128)} %bitcast.2, s32[1,512]{1,0:T(1,128)} %bitcast.3, f32[16,60,240]{2,1,0:T(8,128)} %copy.10.t_ref, f32[4,60,240]{2,1,0:T(8,128)} %copy.11.r_ref, ...), custom_call_target="tpu_custom_call" | custom-call | tf_op jit(solution)/shard_map/pallas_call | solution.py:368
  49.1 1.8 %copy.12 = f32[2,60,512]{2,0,1:T(2,128)} copy(f32[2,60,512]{2,1,0:T(8,128)} %shard_map.82) | data formatting | bytes 491520 | tf_op jit(solution)/shard_map/pallas_call | solution.py:368
Async XLA Ops:
  0.0 3.5 %copy-start = (f32[16,60,240]{2,0,1:T(8,128)S(1)}, f32[16,60,240]{2,0,1:T(8,128)}, u32[]{:S(2)}) copy-start(f32[16,60,240]{2,0,1:T(8,128)} %param.13) | copy-start | bytes 2764804

commit v3 on v2

--- a/solution.py
+++ b/solution.py
@@ -28,13 +28,13 @@
 
 def kernel(
     cells, subs,
-    dir_ref, nbr_ref, spc_ref, kind_ref, box_ref, t_ref, r_ref, cm_ref, out_ref,
-    ext, gown, gall, rall, inc, wts, nls, w2, y2, tpad, dfull, dh, dl, rh, rl, ffull,
+    raw_ref, nbr_ref, spc_ref, kind_ref, box_ref, t_ref, r_ref, cm_ref, out_ref,
+    dir_ref, ext, gown, gall, rall, inc, wts, nls, w2, y2, tpad, dfull, dh, dl, rh, rl, ffull,
     dir_send, dir_recv, halo_send, halo_recv, r_send, r_recv, g_send, g_recv, inc_send, inc_recv,
 ):
-    nrhs, rows, atoms = dir_ref.shape
-    nb, terms = nbr_ref.shape[0], t_ref.shape[0]
-    types, full = r_ref.shape[0], r_ref.shape[2]
+    rows, nrhs, atoms = raw_ref.shape
+    nb, terms = nbr_ref.shape[0], t_ref.shape[1]
+    types, full = r_ref.shape[1], r_ref.shape[2]
     blocks = atoms // BLK
     span = BLK + 2 * WIN
     pad = 64
@@ -55,6 +55,9 @@
             return carry
         lax.fori_loop(0, cells, step, 0)
 
+    for k in range(nrhs):
+        dir_ref[k] = raw_ref[:, k, :]
+
     barrier = pltpu.get_barrier_semaphore()
 
     def greet(to_cell, to_sub):
@@ -136,7 +139,7 @@
 
     rall[cell] = jnp.zeros((types * pad, full), F32)
     for t in range(types):
-        rall[cell, t * pad:t * pad + rows, :] = r_ref[t]
+        rall[cell, t * pad:t * pad + rows, :] = r_ref[:, t, :]
     for way, present in ((0, has_right), (1, has_left)):
         @pl.when(present)
         def _():
@@ -193,15 +196,15 @@
         if b == blocks // 2:
             relay(1)
 
+    hop(1)
     tpad[...] = jnp.zeros_like(tpad)
     for q in range(terms):
-        tpad[q * pad:q * pad + rows, :] = t_ref[q]
+        tpad[q * pad:q * pad + rows, :] = t_ref[:, q, :]
 
     for part, present in parts_there:
         @pl.when(present)
         def _():
             relay(part)
-    hop(1)
     for origin in (mate, cross):
         rows_copy(1, 0, origin).wait_recv()
     for s in range(subs):
@@ -241,6 +244,9 @@
             dh[k, :, lanes] = high
             dl[k, :, lanes] = low
 
+    if cells > 2:
+        hop(2)
+
     per = 4
     for q0 in range(0, terms, per):
         th, tl = split(tpad[q0 * pad:(q0 + per) * pad, :])
@@ -249,9 +255,6 @@
             for q in range(per):
                 y2[q0 + q, k * pad:(k + 1) * pad, :] = high[q * pad:(q + 1) * pad]
                 y2[q0 + q, (nrhs + k) * pad:(nrhs + k + 1) * pad, :] = low[q * pad:(q + 1) * pad]
-
-    if cells > 2:
-        hop(2)
 
     def wait_g(other):
         copy(gown, gall.at[other], g_send.at[other], g_recv.at[other], other, sub).wait_recv()
@@ -325,7 +328,7 @@
         else:
             total = lax.fori_loop(0, cells, apply, total)
         for k in range(nrhs):
-            out_ref[k, :, lanes] = dir_ref[k, :, lanes] - total[:rows, k * BLK:(k + 1) * BLK]
+            out_ref[:, k, lanes] = dir_ref[k, :, lanes] - total[:rows, k * BLK:(k + 1) * BLK]
 
     for way in range(3):
         rows_copy(1, way, sub).wait_send()
@@ -365,12 +368,13 @@
     blocks = atoms // BLK
     span, reach, pad = BLK + 2 * WIN, atoms + 2 * WIN, 64
     dma = pltpu.SemaphoreType.DMA
-    return pl.pallas_call(
+    product = pl.pallas_call(
         functools.partial(kernel, cells, subs),
-        out_shape=jax.ShapeDtypeStruct(direction.shape, F32),
+        out_shape=jax.ShapeDtypeStruct((rows, nrhs, atoms), F32),
         in_specs=[pl.BlockSpec(memory_space=pltpu.VMEM)] * 8,
         out_specs=pl.BlockSpec(memory_space=pltpu.VMEM),
         scratch_shapes=[
+            pltpu.VMEM((nrhs, rows, atoms), F32),
             pltpu.VMEM((subs, nrhs, rows, reach), F32),
             pltpu.VMEM((nrhs * pad, BOX_DEV), F32),
             pltpu.VMEM((cells, nrhs * pad, BOX_DEV), F32),
@@ -395,9 +399,10 @@
             collective_id=0, has_side_effects=True, vmem_limit_bytes=56 * 1024 * 1024
         ),
     )(
-        direction, neighbours, spacing, scatterer.reshape(1, atoms), box_index.reshape(1, atoms),
-        translation, response, coarse_map,
+        jnp.transpose(direction, (1, 0, 2)), neighbours, spacing, scatterer.reshape(1, atoms), box_index.reshape(1, atoms),
+        jnp.transpose(translation, (1, 0, 2)), jnp.transpose(response, (1, 0, 2)), coarse_map,
     )
+    return jnp.transpose(product, (1, 0, 2))
 
 
 def solution(mesh):

time: 51.2 us -> 46.3 us (0.904)
  local copies, waits for them, and re-layouts: 6.89 us -> 1.65 us
    unnamed x5 -> x1, local copies, waits for them, and re-layouts: 5.06 us -> 1.65 us
    pallas_call x1 -> x0, local copies, waits for them, and re-layouts: 1.83 us -> none  [on_device(): pl.pallas_call(functools.partial(kernel, cells, subs), out_shape=jax.Shap...]
where the time goes in v3:
time: 46.3 us; the launch traced here: 46.1 us
  Pallas kernels  44.5 us (96%)
  local copies, waits for them, and re-layouts  1.65 us (4%)
    pallas_call x1, Pallas kernels, on_device(): pl.pallas_call(functools.partial(kernel, cells, subs), out_shape=jax.Shap...  44.5 us
    unnamed x1, local copies, waits for them, and re-layouts  1.65 us

profile of v3, /device:TPU:0, one launch (start us, length us, event | category | flops | bytes accessed | tf_op | source)
XLA Modules:
  0.0 46.1 jit_solution(1715173628468028498)
XLA Ops:
  0.0 44.5 %shard_map.82 = f32[60,2,512]{2,1,0:T(2,128)} custom-call(f32[60,2,512]{2,1,0:T(2,128)} %bitcast.8, s32[12,512]{1,0:T(8,128)} %nbr_ref.1, f32[12,512]{1,0:T(8,128)} %spc_ref.1, s32[1,512]{1,0:T(1,128)} %bitcast.10, s32[1,512]{1,0:T(1,128)} %bitcast.11, f32[60,16,240]{2,1,0:T(8,128)} %bitcast.7, f32[60,4,240]{2,1,0:T(4,128)} %bitcast.9, f32[60,240]{1,0:T(8,128)} %cm_ref.1), custom_call_target="tpu_custom_call" | custom-call | tf_op jit(solution)/shard_map/pallas_call | solution.py:371
  44.5 1.7 %copy.10 = f32[2,60,512]{2,0,1:T(2,128)} copy(f32[2,60,512]{2,0,1:T(2,128)} %bitcast.6) | data formatting | bytes 491520

commit v4 on v3

--- a/solution.py
+++ b/solution.py
@@ -196,15 +196,15 @@
         if b == blocks // 2:
             relay(1)
 
+    for part, present in parts_there:
+        @pl.when(present)
+        def _():
+            relay(part)
     hop(1)
     tpad[...] = jnp.zeros_like(tpad)
     for q in range(terms):
         tpad[q * pad:q * pad + rows, :] = t_ref[:, q, :]
 
-    for part, present in parts_there:
-        @pl.when(present)
-        def _():
-            relay(part)
     for origin in (mate, cross):
         rows_copy(1, 0, origin).wait_recv()
     for s in range(subs):
@@ -230,6 +230,27 @@
     each_far_cell(lambda other: g_copy(other).start())
     gall[cell] = gown[...]
 
+    per = 4
+
+    def translate(lanes):
+        for q0 in range(0, terms, per):
+            th, tl = split(tpad[q0 * pad:(q0 + per) * pad, :])
+            for k in range(nrhs):
+                right = [jnp.concatenate([d[k, :, part] for part in lanes], axis=1) for d in (dh, dl)]
+                high, low = split(dot3(th, tl, *right))
+                at = 0
+                for part in lanes:
+                    here = slice(at, at + part.stop - part.start)
+                    at = here.stop
+                    for q in range(per):
+                        own = slice(q * pad, (q + 1) * pad)
+                        y2[q0 + q, k * pad:(k + 1) * pad, part] = high[own, here]
+                        y2[q0 + q, (nrhs + k) * pad:(nrhs + k + 1) * pad, part] = low[own, here]
+
+    translate([slice(WIN, WIN + atoms)])
+    if cells > 2:
+        hop(2)
+
     for part, present in parts_there:
         @pl.when(present)
         def _():
@@ -244,17 +265,7 @@
             dh[k, :, lanes] = high
             dl[k, :, lanes] = low
 
-    if cells > 2:
-        hop(2)
-
-    per = 4
-    for q0 in range(0, terms, per):
-        th, tl = split(tpad[q0 * pad:(q0 + per) * pad, :])
-        for k in range(nrhs):
-            high, low = split(dot3(th, tl, dh[k], dl[k]))
-            for q in range(per):
-                y2[q0 + q, k * pad:(k + 1) * pad, :] = high[q * pad:(q + 1) * pad]
-                y2[q0 + q, (nrhs + k) * pad:(nrhs + k + 1) * pad, :] = low[q * pad:(q + 1) * pad]
+    translate([slice(0, WIN), slice(WIN + atoms, atoms + 2 * WIN)])
 
     def wait_g(other):
         copy(gown, gall.at[other], g_send.at[other], g_recv.at[other], other, sub).wait_recv()

time: 46.3 us -> 45.9 us (level)
  no operation moved by 1% of the time
where the time goes in v4:
time: 45.9 us; the launch traced here: 45.8 us
  Pallas kernels  44.1 us (96%)
  local copies, waits for them, and re-layouts  1.65 us (4%)
    pallas_call x1, Pallas kernels, on_device(): pl.pallas_call(functools.partial(kernel, cells, subs), out_shape=jax.Shap...  44.1 us
    unnamed x1, local copies, waits for them, and re-layouts  1.65 us

profile of v4, /device:TPU:0, one launch (start us, length us, event | category | flops | bytes accessed | tf_op | source)
XLA Modules:
  0.0 45.8 jit_solution(2537876413338450868)
XLA Ops:
  0.0 44.1 %shard_map.82 = f32[60,2,512]{2,1,0:T(2,128)} custom-call(f32[60,2,512]{2,1,0:T(2,128)} %bitcast.8, s32[12,512]{1,0:T(8,128)} %nbr_ref.1, f32[12,512]{1,0:T(8,128)} %spc_ref.1, s32[1,512]{1,0:T(1,128)} %bitcast.10, s32[1,512]{1,0:T(1,128)} %bitcast.11, f32[60,16,240]{2,1,0:T(8,128)} %bitcast.7, f32[60,4,240]{2,1,0:T(4,128)} %bitcast.9, f32[60,240]{1,0:T(8,128)} %cm_ref.1), custom_call_target="tpu_custom_call" | custom-call | tf_op jit(solution)/shard_map/pallas_call | solution.py:382
  44.1 1.7 %copy.10 = f32[2,60,512]{2,0,1:T(2,128)} copy(f32[2,60,512]{2,0,1:T(2,128)} %bitcast.6) | data formatting | bytes 491520
